TPU v7x, 256 devices: a whole 4x4x8 slice. The times are simulated.
256 devices in a mesh: sta: 64 (over z_hi, y, x), freq: 4 (over z_lo, core).
Axes of the slice: x: 4, y: 4, z: 8 (z_hi: 4, z_lo: 2; z = z_hi * 2 + z_lo), core: 2. Of those that a mesh axis runs over, the one named last changes fastest.
Arguments:
- waveforms: bfloat16 [256, 4, 8192], P('sta'), may hold values from -6 to 6
- fir_taps: float32 [256, 256], P('sta'), may hold values from -0.375 to 0.375
- water_level: float32 [256], P('sta'), may hold values from 0.1 to 1
- gap_start: int32 [256, 4], P('sta'), may hold values from 0 to 8191
- gap_length: int32 [256, 4], P('sta'), may hold values from 0 to 2048
- live_slots: int32 [64], P('sta'), may hold values from 2 to 4, as said below
Outputs:
- correlations: bfloat16 [2, 96, 256, 4, 128], P(None, 'freq', 'sta')
Inputs may be any that keep to these rules, and one draw needn't show every extreme that they name: Block d holds stations in its first live_slots[d] slots; the other slots are empty.
All inputs are finite; a program needn't handle non-finite values.
Results may differ from a plain program's by a relative error of at most 0.018.
Values may be sent and summed in bfloat16 or wider, within the bound.
A program may use at most 192 MiB of HBM per device.

v0:
```python
import functools
import math

import jax
import jax.numpy as jnp
import ml_dtypes
import numpy as np
from jax import lax
from jax.experimental import pallas as pl
from jax.experimental.pallas import tpu as pltpu
from jax.sharding import PartitionSpec as P

ROOT = 128
COARSE = 64
LAGROWS = 96
ROUNDS = 2
SLOTS = 4
SEG = 4
KEPT = 72
BAND = LAGROWS // 4
MESH = pl.DeviceIdType.MESH


def as_bf16(table):
    return table.astype(np.float32).astype(ml_dtypes.bfloat16)


def split_bf16(table):
    upper = as_bf16(table)
    return upper, as_bf16(table - upper.astype(np.float64))


def make_tables():
    kept = np.arange(KEPT)
    live = (kept <= 64).astype(np.float64)[:, None]
    full = np.arange(ROOT)
    angle = 2.0 * math.pi / ROOT
    first = kept[:, None] * np.arange(COARSE)[None, :] * angle
    first = np.concatenate([np.cos(first) * live, -np.sin(first) * live], axis=0)
    first_hi, first_lo = split_bf16(first)
    first_table = np.concatenate([first_hi, first_lo], axis=1)
    twist = kept[:, None] * full[None, :] * (angle / ROOT)
    weight = np.where((kept == 0) | (kept == 64), 1.0, 2.0)[:, None] * live
    weight = weight / math.sqrt(SEG * ROOT * ROOT)
    step = np.broadcast_to(kept[:, None] * angle, (KEPT, ROOT))
    twiddles = np.stack(
        [np.cos(twist), np.sin(twist), np.cos(twist) * weight, np.sin(twist) * weight, np.cos(step), np.sin(step)]
    ).astype(np.float32)
    square = full[:, None] * full[None, :] * angle
    cos_b, sin_b = np.cos(square), np.sin(square)
    last = np.block([[cos_b, -sin_b], [sin_b, cos_b]])
    last_hi, last_lo = split_bf16(last)
    inner = as_bf16(np.block([[cos_b, sin_b], [-sin_b, cos_b]]))
    square_tables = np.stack([last_hi, last_lo, inner])
    lag = (np.arange(LAGROWS) - LAGROWS // 2)[:, None] * kept[None, :] * angle
    outer = as_bf16(np.concatenate([np.cos(lag), -np.sin(lag)], axis=1))
    return first_table, twiddles, square_tables, outer


def dot(left, right):
    return jnp.dot(left, right, preferred_element_type=jnp.float32)


def spectra(wave, about, first_table, twiddles, squares):
    place = (
        lax.broadcasted_iota(jnp.int32, (COARSE, ROOT), 0) * ROOT
        + lax.broadcasted_iota(jnp.int32, (COARSE, ROOT), 1)
    ).astype(jnp.float32)
    records = []
    for s in range(SEG):
        start = about[4 + s : 5 + s, :]
        end = about[8 + s : 9 + s, :]
        gone = (place >= start) & (place < end)
        record = jnp.where(gone, 0.0, wave[s].astype(jnp.float32))
        records.append(record.astype(jnp.bfloat16))
    record = jnp.concatenate(records, axis=1)
    section = dot(first_table, jnp.concatenate([record, record], axis=0))
    cos_t, sin_t = twiddles[0], twiddles[1]
    tap0 = about[0:1, :]
    tap1 = about[1:2, :]
    rows = [(tap0 + tap1 * twiddles[4], -(tap1 * twiddles[5]))]
    for s in range(SEG):
        columns = section[:, s * ROOT : (s + 1) * ROOT]
        rows.append((columns[:KEPT], columns[KEPT:]))
    twisted = jnp.concatenate(
        [
            jnp.concatenate([re * cos_t + im * sin_t, im * cos_t - re * sin_t], axis=1)
            for re, im in rows
        ],
        axis=0,
    )
    upper = twisted.astype(jnp.bfloat16)
    lower = (twisted - upper.astype(jnp.float32)).astype(jnp.bfloat16)
    bins = dot(upper, squares[0]) + dot(lower, squares[0]) + dot(upper, squares[1])
    resp_re, resp_im = bins[:KEPT, :ROOT], bins[:KEPT, ROOT:]
    water = about[2:3, :]
    alive = about[3:4, :]
    found = []
    for s in range(SEG):
        part = bins[(s + 1) * KEPT : (s + 2) * KEPT]
        spec_re, spec_im = part[:, :ROOT], part[:, ROOT:]
        white_re = resp_re * spec_re - resp_im * spec_im
        white_im = resp_re * spec_im + resp_im * spec_re
        factor = alive * lax.rsqrt(white_re * white_re + white_im * white_im + water)
        found.append((white_re * factor, white_im * factor))
    return found


def kernel(
    n_sta,
    wave_ref,
    taps_ref,
    water_ref,
    start_ref,
    length_ref,
    live_ref,
    first_ref,
    twiddle_ref,
    square_ref,
    outer_ref,
    out_ref,
    about_ref,
    far_wave_ref,
    far_about_ref,
    own_ref,
    part_ref,
    got_ref,
    rows_ref,
    send_sem,
    recv_sem,
    part_send_sem,
    part_recv_sem,
):
    sta = lax.axis_index("sta")
    freq = lax.axis_index("freq")
    core = lax.rem(freq, 2)
    upper_chip = freq // 2
    stride = n_sta // (2 * ROUNDS)

    def block(steps):
        return lax.rem(sta + (steps % 4) * stride, n_sta)

    barrier = pltpu.get_barrier_semaphore()
    pl.semaphore_signal(barrier, inc=1, device_id={"sta": block(-1), "freq": 2 + core}, device_id_type=MESH)
    pl.semaphore_signal(
        barrier,
        inc=1,
        device_id={"sta": block(-2), "freq": 2 * (1 - upper_chip) + core},
        device_id_type=MESH,
    )
    for step in range(1, 4):
        pl.semaphore_signal(
            barrier, inc=1, device_id={"sta": sta, "freq": lax.rem(freq + step, 4)}, device_id_type=MESH
        )

    for slot in range(SLOTS):
        about_ref[slot, 0:1, :] = taps_ref[slot : slot + 1, :ROOT]
        about_ref[slot, 1:2, :] = taps_ref[slot : slot + 1, ROOT:]
        about_ref[slot, 2:3, :] = jnp.full((1, ROOT), water_ref[slot] * float(COARSE * ROOT), jnp.float32)
        about_ref[slot, 3:4, :] = jnp.full((1, ROOT), (live_ref[0] > slot).astype(jnp.float32), jnp.float32)
        for s in range(SEG):
            first = start_ref[slot, s]
            after = first + length_ref[slot, s]
            about_ref[slot, 4 + s : 5 + s, :] = jnp.full((1, ROOT), first.astype(jnp.float32), jnp.float32)
            about_ref[slot, 8 + s : 9 + s, :] = jnp.full((1, ROOT), after.astype(jnp.float32), jnp.float32)
        about_ref[slot, 12:16, :] = jnp.zeros((4, ROOT), jnp.float32)

    pl.semaphore_wait(barrier, 4 + 2 * upper_chip)

    def copies(order, slot, buffer, steps, target):
        where = {"sta": block(steps), "freq": target}
        return [
            pltpu.make_async_remote_copy(
                src_ref=src.at[slot],
                dst_ref=dst.at[buffer],
                send_sem=send_sem.at[order, which],
                recv_sem=recv_sem.at[buffer, which],
                device_id=where,
                device_id_type=MESH,
            )
            for which, (src, dst) in enumerate(((about_ref, far_about_ref), (wave_ref, far_wave_ref)))
        ]

    def for_upper():
        return (
            copies(0, core, 0, 1, core)
            + copies(1, 2 + core, 0, 1, 2 + core)
            + copies(2, core, 1, 2, core)
        )

    def for_lower():
        return copies(0, 2 + core, 1, 2, 2 + core)

    @pl.when(upper_chip == 1)
    def _():
        for copy in for_upper():
            copy.start()

    @pl.when(upper_chip == 0)
    def _():
        for copy in for_lower():
            copy.start()

    first_table = first_ref[...]
    outer_table = outer_ref[...]

    def own_step(slot, carry):
        found = spectra(wave_ref[slot], about_ref[slot], first_ref[...], twiddle_ref, square_ref)
        for s in range(SEG):
            own_ref[slot, s, 0], own_ref[slot, s, 1] = found[s]
        return carry

    lax.fori_loop(0, SLOTS, own_step, 0)

    def exchange(round_index, step):
        target = lax.rem(freq + step, 4)
        return pltpu.make_async_remote_copy(
            src_ref=part_ref.at[round_index, target],
            dst_ref=got_ref.at[round_index, freq],
            send_sem=part_send_sem.at[round_index, step],
            recv_sem=part_recv_sem.at[round_index, step],
            device_id={"sta": sta, "freq": target},
            device_id_type=MESH,
        )

    for r in range(ROUNDS):
        for copy in copies(0, 0, r, 0, 0):
            copy.wait_recv()
        far = spectra(far_wave_ref[r], far_about_ref[r], first_table, twiddle_ref, square_ref)
        pairs = []
        for i in range(SLOTS):
            cross_re = 0.0
            cross_im = 0.0
            for s in range(SEG):
                own_re, own_im = own_ref[i, s, 0], own_ref[i, s, 1]
                far_re, far_im = far[s]
                cross_re = cross_re + own_re * far_re + own_im * far_im
                cross_im = cross_im + own_im * far_re - own_re * far_im
            pairs.append(jnp.concatenate([cross_re, cross_im], axis=1))
        inner = dot(jnp.concatenate(pairs, axis=0).astype(jnp.bfloat16), square_ref[2])
        columns = []
        for i in range(SLOTS):
            inner_re = inner[i * KEPT : (i + 1) * KEPT, :ROOT]
            inner_im = inner[i * KEPT : (i + 1) * KEPT, ROOT:]
            cos_t, sin_t = twiddle_ref[2], twiddle_ref[3]
            columns.append(
                jnp.concatenate(
                    [inner_re * cos_t - inner_im * sin_t, inner_re * sin_t + inner_im * cos_t], axis=0
                ).astype(jnp.bfloat16)
            )
        lagged = dot(outer_table, jnp.concatenate(columns, axis=1))
        for g in range(4):
            band = lagged[g * BAND : (g + 1) * BAND]
            part_ref[r, g] = jnp.concatenate(
                [band[:, i * ROOT : (i + 1) * ROOT] for i in range(SLOTS)], axis=0
            ).astype(jnp.bfloat16)
        for step in (2, 1, 3):
            exchange(r, step).start()
        got_ref[r, freq] = part_ref[r, freq]

    for r in range(ROUNDS):
        for step in (1, 2, 3):
            exchange(r, step).wait_recv()
        for j in range(SLOTS):
            piece = got_ref[r, j].astype(jnp.float32)
            for i in range(SLOTS):
                rows_ref[r, pl.ds(SLOTS * i + j, BAND, stride=SLOTS * SLOTS), :] = piece[i * BAND : (i + 1) * BAND]
        out_ref[r] = rows_ref[r].astype(jnp.bfloat16)

    for r in range(ROUNDS):
        for step in (1, 2, 3):
            exchange(r, step).wait_send()

    @pl.when(upper_chip == 1)
    def _():
        for copy in for_upper():
            copy.wait_send()

    @pl.when(upper_chip == 0)
    def _():
        for copy in for_lower():
            copy.wait_send()


def on_device(waveforms, fir_taps, water_level, gap_start, gap_length, live_slots):
    n_sta = lax.axis_size("sta")
    tables = [jnp.asarray(table) for table in make_tables()]
    wave = waveforms.reshape(SLOTS, SEG, COARSE, ROOT)
    vmem = pl.BlockSpec(memory_space=pltpu.VMEM)
    smem = pl.BlockSpec(memory_space=pltpu.SMEM)
    rows = BAND * SLOTS * SLOTS
    result = pl.pallas_call(
        functools.partial(kernel, n_sta),
        out_shape=jax.ShapeDtypeStruct((ROUNDS, rows, ROOT), jnp.bfloat16),
        in_specs=[vmem, vmem, smem, smem, smem, smem, vmem, vmem, vmem, vmem],
        out_specs=vmem,
        scratch_shapes=[
            pltpu.VMEM((SLOTS, 16, ROOT), jnp.float32),
            pltpu.VMEM((ROUNDS, SEG, COARSE, ROOT), jnp.bfloat16),
            pltpu.VMEM((ROUNDS, 16, ROOT), jnp.float32),
            pltpu.VMEM((SLOTS, SEG, 2, KEPT, ROOT), jnp.float32),
            pltpu.VMEM((ROUNDS, 4, SLOTS * BAND, ROOT), jnp.bfloat16),
            pltpu.VMEM((ROUNDS, 4, SLOTS * BAND, ROOT), jnp.bfloat16),
            pltpu.VMEM((ROUNDS, rows, ROOT), jnp.float32),
            pltpu.SemaphoreType.DMA((3, 2)),
            pltpu.SemaphoreType.DMA((ROUNDS, 2)),
            pltpu.SemaphoreType.DMA((ROUNDS, 4)),
            pltpu.SemaphoreType.DMA((ROUNDS, 4)),
        ],
        compiler_params=pltpu.CompilerParams(
            collective_id=0, has_side_effects=True, vmem_limit_bytes=40 * 1024 * 1024
        ),
    )(wave, fir_taps, water_level, gap_start, gap_length, live_slots, *tables)
    return result.reshape(ROUNDS, BAND, SLOTS, SLOTS, ROOT)


def solution(mesh):
    in_specs = (
        P("sta", None, None),
        P("sta", None),
        P("sta"),
        P("sta", None),
        P("sta", None),
        P("sta"),
    )
    out_specs = P(None, "freq", "sta", None, None)
    return jax.shard_map(
        on_device, mesh=mesh, in_specs=in_specs, out_specs=out_specs, check_vma=False
    )
```

profile of v0, /device:TPU:1, one launch (start us, length us, event | category | flops | bytes accessed | tf_op | source)
XLA Modules:
  0.0 23.2 jit_solution(16558712503755059924)
XLA Ops:
  0.0 0.0 copy-start
  0.7 0.0 copy-start.2
  0.7 0.0 copy-start.3
  0.7 0.0 copy-start.4
  0.7 0.0 copy-start.5
  0.8 0.0 copy-start.6
  0.8 0.0 copy-start.7
  0.8 1.3 %reshape.6.wave_ref = bf16[4,4,64,128]{3,2,1,0:T(8,128)(2,1)S(1)} reshape(bf16[4,4,8192]{2,1,0:T(4,128)(2,1)} %param.10) | data formatting | bytes 524288 | tf_op jit(solution)/shard_map/reshape | solution.py:288
  2.0 0.0 copy-done
  2.1 0.0 copy-done.2
  2.1 0.0 copy-done.3
  2.1 0.0 copy-done.4
  2.1 0.0 copy-done.5
  2.1 0.0 copy-done.6
  2.1 0.0 copy-done.7
  2.1 0.0 copy-start.1
  2.1 0.9 %copy-done.1 = f32[6,72,128]{2,1,0:T(8,128)S(1)} copy-done((f32[6,72,128]{2,1,0:T(8,128)S(1)}, f32[6,72,128]{2,1,0:T(8,128)}, u32[]{:S(2)}) %copy-start.1) | copy-done | bytes 221208
  3.1 19.4 %shard_map.100 = bf16[2,384,128]{2,1,0:T(8,128)(2,1)S(1)} custom-call(bf16[4,4,64,128]{3,2,1,0:T(8,128)(2,1)S(1)} %reshape.6.wave_ref, f32[4,256]{1,0:T(4,128)S(1)} %copy-done.4, f32[4]{0:T(128)S(1)} %copy-done.7, s32[4,4]{1,0:T(4,128)S(1)} %copy-done.5, s32[4,4]{1,0:T(4,128)S(1)} %copy-done.6, s32[1]{0:T(128)S(6)} %copy.12.live_ref, ...), custom_call_target="tpu_custom_call" | custom-call | tf_op jit(solution)/shard_map/pallas_call | solution.py:292
  22.5 0.7 %copy.13 = bf16[2,24,4,4,128]{4,3,2,1,0:T(4,128)(2,1)} copy(bf16[2,24,4,4,128]{4,3,2,1,0:T(4,128)(2,1)S(1)} %bitcast.1) | data formatting | bytes 393216
Async XLA Ops:
  0.0 2.1 %copy-start = (bf16[3,256,256]{2,1,0:T(8,128)(2,1)S(1)}, bf16[3,256,256]{2,1,0:T(8,128)(2,1)}, u32[]{:S(2)}) copy-start(bf16[3,256,256]{2,1,0:T(8,128)(2,1)} %constant.10.clone.square_ref) | copy-start | bytes 1179652
  0.7 1.4 %copy-start.2 = (bf16[96,144]{1,0:T(8,128)(2,1)S(1)}, bf16[96,144]{1,0:T(8,128)(2,1)}, u32[]{:S(2)}) copy-start(bf16[96,144]{1,0:T(8,128)(2,1)} %constant.11.clone.outer_ref) | copy-start | bytes 82948
  0.7 1.4 %copy-start.3 = (bf16[144,128]{1,0:T(8,128)(2,1)S(1)}, bf16[144,128]{1,0:T(8,128)(2,1)}, u32[]{:S(2)}) copy-start(bf16[144,128]{1,0:T(8,128)(2,1)} %constant.8.clone.first_ref) | copy-start | bytes 110596
  0.7 1.4 %copy-start.4 = (f32[4,256]{1,0:T(4,128)S(1)}, f32[4,256]{1,0:T(4,128)}, u32[]{:S(2)}) copy-start(f32[4,256]{1,0:T(4,128)} %taps_ref.1) | copy-start | bytes 12292
  0.7 1.4 %copy-start.5 = (s32[4,4]{1,0:T(4,128)S(1)}, s32[4,4]{1,0:T(4,128)}, u32[]{:S(2)}) copy-start(s32[4,4]{1,0:T(4,128)} %start_ref.1) | copy-start | bytes 196
  0.8 1.4 %copy-start.6 = (s32[4,4]{1,0:T(4,128)S(1)}, s32[4,4]{1,0:T(4,128)}, u32[]{:S(2)}) copy-start(s32[4,4]{1,0:T(4,128)} %length_ref.1) | copy-start | bytes 196
  0.8 1.4 %copy-start.7 = (f32[4]{0:T(128)S(1)}, f32[4]{0:T(128)}, u32[]{:S(2)}) copy-start(f32[4]{0:T(128)} %water_ref.1) | copy-start | bytes 52
  2.1 0.9 %copy-start.1 = (f32[6,72,128]{2,1,0:T(8,128)S(1)}, f32[6,72,128]{2,1,0:T(8,128)}, u32[]{:S(2)}) copy-start(f32[6,72,128]{2,1,0:T(8,128)} %constant.9.clone.twiddle_ref) | copy-start | bytes 663556
where the time goes:
time: 23.3 us; the launch traced here: 23.2 us
  Pallas kernels  19.4 us (83%)
  local copies, waits for them, and re-layouts  2.92 us (13%)
  between operations  0.83 us (4%)
    pallas_call x1, Pallas kernels, on_device(): pl.pallas_call(functools.partial(kernel, n_sta), out_shape=jax.ShapeDtype...  19.4 us
    unnamed x17, local copies, waits for them, and re-layouts  1.65 us
    reshape x1, local copies, waits for them, and re-layouts, on_device(): wave = waveforms.reshape(SLOTS, SEG, COARSE, ROOT)  1.27 us

commit v1 on v0

--- a/solution.py
+++ b/solution.py
@@ -61,17 +61,20 @@
     return jnp.dot(left, right, preferred_element_type=jnp.float32)
 
 
-def spectra(wave, about, first_table, twiddles, squares):
+def spectra(wave, about, stage, first_table, twiddles, squares):
     place = (
         lax.broadcasted_iota(jnp.int32, (COARSE, ROOT), 0) * ROOT
         + lax.broadcasted_iota(jnp.int32, (COARSE, ROOT), 1)
     ).astype(jnp.float32)
+    wide = wave.astype(jnp.float32)
+    for row in range(COARSE):
+        stage[SEG * row : SEG * (row + 1), :] = wide[:, row * ROOT : (row + 1) * ROOT]
     records = []
     for s in range(SEG):
         start = about[4 + s : 5 + s, :]
         end = about[8 + s : 9 + s, :]
         gone = (place >= start) & (place < end)
-        record = jnp.where(gone, 0.0, wave[s].astype(jnp.float32))
+        record = jnp.where(gone, 0.0, stage[pl.ds(s, COARSE, stride=SEG), :])
         records.append(record.astype(jnp.bfloat16))
     record = jnp.concatenate(records, axis=1)
     section = dot(first_table, jnp.concatenate([record, record], axis=0))
@@ -108,6 +111,17 @@
 
 def kernel(
     n_sta,
+    wave_hbm,
+    taps_hbm,
+    water_hbm,
+    start_hbm,
+    length_hbm,
+    live_hbm,
+    first_hbm,
+    twiddle_hbm,
+    square_hbm,
+    outer_hbm,
+    out_ref,
     wave_ref,
     taps_ref,
     water_ref,
@@ -118,14 +132,15 @@
     twiddle_ref,
     square_ref,
     outer_ref,
-    out_ref,
     about_ref,
     far_wave_ref,
     far_about_ref,
+    stage_ref,
     own_ref,
     part_ref,
     got_ref,
     rows_ref,
+    load_sem,
     send_sem,
     recv_sem,
     part_send_sem,
@@ -141,17 +156,70 @@
         return lax.rem(sta + (steps % 4) * stride, n_sta)
 
     barrier = pltpu.get_barrier_semaphore()
-    pl.semaphore_signal(barrier, inc=1, device_id={"sta": block(-1), "freq": 2 + core}, device_id_type=MESH)
-    pl.semaphore_signal(
-        barrier,
-        inc=1,
-        device_id={"sta": block(-2), "freq": 2 * (1 - upper_chip) + core},
-        device_id_type=MESH,
-    )
-    for step in range(1, 4):
+    for steps, source in ((-1, 2), (-1, 3), (-2, 0), (-2, 1)):
         pl.semaphore_signal(
-            barrier, inc=1, device_id={"sta": sta, "freq": lax.rem(freq + step, 4)}, device_id_type=MESH
-        )
+            barrier, inc=1, device_id={"sta": block(steps), "freq": source}, device_id_type=MESH
+        )
+
+    small = [
+        pltpu.make_async_copy(source, target, load_sem.at[n])
+        for n, (source, target) in enumerate(
+            (
+                (taps_hbm, taps_ref),
+                (water_hbm, water_ref),
+                (start_hbm, start_ref),
+                (length_hbm, length_ref),
+                (live_hbm, live_ref),
+            )
+        )
+    ]
+    large = [
+        pltpu.make_async_copy(source, target, load_sem.at[5 + n])
+        for n, (source, target) in enumerate(
+            (
+                (wave_hbm, wave_ref),
+                (first_hbm, first_ref),
+                (twiddle_hbm, twiddle_ref),
+                (square_hbm, square_ref),
+                (outer_hbm, outer_ref),
+            )
+        )
+    ]
+    for copy in small + large:
+        copy.start()
+
+    pl.semaphore_wait(barrier, 4)
+
+    feeds = {"sta": lax.rem(sta + (2 - upper_chip) * stride, n_sta), "freq": 2 * (1 - upper_chip) + core}
+
+    def send_wave(q):
+        return pltpu.make_async_remote_copy(
+            src_ref=wave_hbm.at[2 * core + q],
+            dst_ref=far_wave_ref.at[q],
+            send_sem=send_sem.at[q],
+            recv_sem=recv_sem.at[q],
+            device_id=feeds,
+            device_id_type=MESH,
+        )
+
+    def send_about():
+        return pltpu.make_async_remote_copy(
+            src_ref=about_ref.at[pl.ds(2 * core, 2)],
+            dst_ref=far_about_ref,
+            send_sem=send_sem.at[2],
+            recv_sem=recv_sem.at[2],
+            device_id=feeds,
+            device_id_type=MESH,
+        )
+
+    waits = (1 - upper_chip) * lax.rem(sta // stride, 2)
+
+    @pl.when(waits == 0)
+    def _():
+        send_wave(0).start()
+
+    for copy in small:
+        copy.wait()
 
     for slot in range(SLOTS):
         about_ref[slot, 0:1, :] = taps_ref[slot : slot + 1, :ROOT]
@@ -165,68 +233,51 @@
             about_ref[slot, 8 + s : 9 + s, :] = jnp.full((1, ROOT), after.astype(jnp.float32), jnp.float32)
         about_ref[slot, 12:16, :] = jnp.zeros((4, ROOT), jnp.float32)
 
-    pl.semaphore_wait(barrier, 4 + 2 * upper_chip)
-
-    def copies(order, slot, buffer, steps, target):
-        where = {"sta": block(steps), "freq": target}
-        return [
-            pltpu.make_async_remote_copy(
-                src_ref=src.at[slot],
-                dst_ref=dst.at[buffer],
-                send_sem=send_sem.at[order, which],
-                recv_sem=recv_sem.at[buffer, which],
-                device_id=where,
-                device_id_type=MESH,
-            )
-            for which, (src, dst) in enumerate(((about_ref, far_about_ref), (wave_ref, far_wave_ref)))
-        ]
-
-    def for_upper():
-        return (
-            copies(0, core, 0, 1, core)
-            + copies(1, 2 + core, 0, 1, 2 + core)
-            + copies(2, core, 1, 2, core)
-        )
-
-    def for_lower():
-        return copies(0, 2 + core, 1, 2, 2 + core)
-
-    @pl.when(upper_chip == 1)
+    @pl.when(waits == 0)
     def _():
-        for copy in for_upper():
-            copy.start()
-
-    @pl.when(upper_chip == 0)
-    def _():
-        for copy in for_lower():
-            copy.start()
+        send_about().start()
+        send_wave(1).start()
+
+    for copy in large:
+        copy.wait()
 
     first_table = first_ref[...]
     outer_table = outer_ref[...]
 
     def own_step(slot, carry):
-        found = spectra(wave_ref[slot], about_ref[slot], first_ref[...], twiddle_ref, square_ref)
+        found = spectra(
+            wave_ref[slot], about_ref[slot], stage_ref, first_ref[...], twiddle_ref, square_ref
+        )
         for s in range(SEG):
             own_ref[slot, s, 0], own_ref[slot, s, 1] = found[s]
         return carry
 
     lax.fori_loop(0, SLOTS, own_step, 0)
 
-    def exchange(round_index, step):
+    @pl.when(waits == 1)
+    def _():
+        send_wave(0).start()
+        send_about().start()
+        send_wave(1).start()
+
+    def exchange(q, step):
         target = lax.rem(freq + step, 4)
         return pltpu.make_async_remote_copy(
-            src_ref=part_ref.at[round_index, target],
-            dst_ref=got_ref.at[round_index, freq],
-            send_sem=part_send_sem.at[round_index, step],
-            recv_sem=part_recv_sem.at[round_index, step],
+            src_ref=part_ref.at[q, target],
+            dst_ref=got_ref.at[upper_chip, 2 * core + q],
+            send_sem=part_send_sem.at[q, step],
+            recv_sem=part_recv_sem.at[q, step],
             device_id={"sta": sta, "freq": target},
             device_id_type=MESH,
         )
 
-    for r in range(ROUNDS):
-        for copy in copies(0, 0, r, 0, 0):
-            copy.wait_recv()
-        far = spectra(far_wave_ref[r], far_about_ref[r], first_table, twiddle_ref, square_ref)
+    for q in range(2):
+        if q == 0:
+            pltpu.make_async_copy(far_about_ref, far_about_ref, recv_sem.at[2]).wait()
+        pltpu.make_async_copy(far_wave_ref.at[q], far_wave_ref.at[q], recv_sem.at[q]).wait()
+        far = spectra(
+            far_wave_ref[q], far_about_ref[q], stage_ref, first_table, twiddle_ref, square_ref
+        )
         pairs = []
         for i in range(SLOTS):
             cross_re = 0.0
@@ -251,66 +302,68 @@
         lagged = dot(outer_table, jnp.concatenate(columns, axis=1))
         for g in range(4):
             band = lagged[g * BAND : (g + 1) * BAND]
-            part_ref[r, g] = jnp.concatenate(
+            part_ref[q, g] = jnp.concatenate(
                 [band[:, i * ROOT : (i + 1) * ROOT] for i in range(SLOTS)], axis=0
             ).astype(jnp.bfloat16)
         for step in (2, 1, 3):
-            exchange(r, step).start()
-        got_ref[r, freq] = part_ref[r, freq]
-
+            exchange(q, step).start()
+        got_ref[upper_chip, 2 * core + q] = part_ref[q, freq]
+
+    for q in range(2):
+        for step in (1, 2, 3):
+            exchange(q, step).wait_recv()
     for r in range(ROUNDS):
-        for step in (1, 2, 3):
-            exchange(r, step).wait_recv()
         for j in range(SLOTS):
             piece = got_ref[r, j].astype(jnp.float32)
             for i in range(SLOTS):
                 rows_ref[r, pl.ds(SLOTS * i + j, BAND, stride=SLOTS * SLOTS), :] = piece[i * BAND : (i + 1) * BAND]
         out_ref[r] = rows_ref[r].astype(jnp.bfloat16)
 
-    for r in range(ROUNDS):
+    for q in range(2):
         for step in (1, 2, 3):
-            exchange(r, step).wait_send()
-
-    @pl.when(upper_chip == 1)
-    def _():
-        for copy in for_upper():
-            copy.wait_send()
-
-    @pl.when(upper_chip == 0)
-    def _():
-        for copy in for_lower():
-            copy.wait_send()
+            exchange(q, step).wait_send()
+        send_wave(q).wait_send()
+    send_about().wait_send()
 
 
 def on_device(waveforms, fir_taps, water_level, gap_start, gap_length, live_slots):
     n_sta = lax.axis_size("sta")
     tables = [jnp.asarray(table) for table in make_tables()]
-    wave = waveforms.reshape(SLOTS, SEG, COARSE, ROOT)
-    vmem = pl.BlockSpec(memory_space=pltpu.VMEM)
-    smem = pl.BlockSpec(memory_space=pltpu.SMEM)
+    anywhere = pl.BlockSpec(memory_space=pl.ANY)
     rows = BAND * SLOTS * SLOTS
     result = pl.pallas_call(
         functools.partial(kernel, n_sta),
         out_shape=jax.ShapeDtypeStruct((ROUNDS, rows, ROOT), jnp.bfloat16),
-        in_specs=[vmem, vmem, smem, smem, smem, smem, vmem, vmem, vmem, vmem],
-        out_specs=vmem,
+        in_specs=[anywhere] * 10,
+        out_specs=pl.BlockSpec(memory_space=pltpu.VMEM),
         scratch_shapes=[
+            pltpu.VMEM((SLOTS, SEG, COARSE * ROOT), jnp.bfloat16),
+            pltpu.VMEM((SLOTS, 2 * ROOT), jnp.float32),
+            pltpu.SMEM((SLOTS,), jnp.float32),
+            pltpu.SMEM((SLOTS, SEG), jnp.int32),
+            pltpu.SMEM((SLOTS, SEG), jnp.int32),
+            pltpu.SMEM((1,), jnp.int32),
+        ]
+        + [pltpu.VMEM(table.shape, table.dtype) for table in tables]
+        + [
             pltpu.VMEM((SLOTS, 16, ROOT), jnp.float32),
-            pltpu.VMEM((ROUNDS, SEG, COARSE, ROOT), jnp.bfloat16),
-            pltpu.VMEM((ROUNDS, 16, ROOT), jnp.float32),
+            pltpu.VMEM((2, SEG, COARSE * ROOT), jnp.bfloat16),
+            pltpu.VMEM((2, 16, ROOT), jnp.float32),
+            pltpu.VMEM((SEG * COARSE, ROOT), jnp.float32),
             pltpu.VMEM((SLOTS, SEG, 2, KEPT, ROOT), jnp.float32),
-            pltpu.VMEM((ROUNDS, 4, SLOTS * BAND, ROOT), jnp.bfloat16),
-            pltpu.VMEM((ROUNDS, 4, SLOTS * BAND, ROOT), jnp.bfloat16),
+            pltpu.VMEM((2, 4, SLOTS * BAND, ROOT), jnp.bfloat16),
+            pltpu.VMEM((ROUNDS, SLOTS, SLOTS * BAND, ROOT), jnp.bfloat16),
             pltpu.VMEM((ROUNDS, rows, ROOT), jnp.float32),
-            pltpu.SemaphoreType.DMA((3, 2)),
-            pltpu.SemaphoreType.DMA((ROUNDS, 2)),
-            pltpu.SemaphoreType.DMA((ROUNDS, 4)),
-            pltpu.SemaphoreType.DMA((ROUNDS, 4)),
+            pltpu.SemaphoreType.DMA((10,)),
+            pltpu.SemaphoreType.DMA((3,)),
+            pltpu.SemaphoreType.DMA((3,)),
+            pltpu.SemaphoreType.DMA((2, 4)),
+            pltpu.SemaphoreType.DMA((2, 4)),
         ],
         compiler_params=pltpu.CompilerParams(
-            collective_id=0, has_side_effects=True, vmem_limit_bytes=40 * 1024 * 1024
+            collective_id=0, has_side_effects=True, vmem_limit_bytes=56 * 1024 * 1024
         ),
-    )(wave, fir_taps, water_level, gap_start, gap_length, live_slots, *tables)
+    )(waveforms, fir_taps, water_level, gap_start, gap_length, live_slots, *tables)
     return result.reshape(ROUNDS, BAND, SLOTS, SLOTS, ROOT)
 
 

time: 23.3 us -> 23.7 us (1.017)
  the two profiles are of different devices: /device:TPU:1 before, /device:TPU:65 now
where the time goes in v1:
time: 23.7 us; the launch traced here: 23.6 us
  Pallas kernels  21.2 us (89%)
  local copies, waits for them, and re-layouts  1.67 us (7%)
  between operations  0.66 us (3%)
    pallas_call x1, Pallas kernels, on_device(): pl.pallas_call(functools.partial(kernel, n_sta), out_shape=jax.ShapeDtype...  21.2 us
    unnamed x1, local copies, waits for them, and re-layouts  1.67 us

profile of v1, /device:TPU:65, one launch (start us, length us, event | category | flops | bytes accessed | tf_op | source)
XLA Modules:
  0.0 23.6 jit_solution(4916487913880269908)
XLA Ops:
  0.7 21.2 %shard_map.100 = bf16[2,384,128]{2,1,0:T(8,128)(2,1)} custom-call(bf16[4,4,8192]{2,1,0:T(4,128)(2,1)} %wave_hbm.1, f32[4,256]{1,0:T(4,128)} %taps_hbm.1, f32[4]{0:T(128)} %water_hbm.1, s32[4,4]{1,0:T(4,128)} %start_hbm.1, s32[4,4]{1,0:T(4,128)} %length_hbm.1, s32[1]{0:T(128)S(6)} %copy.12.live_hbm, bf16[144,128]{1,0:T(8,128)(2,1)} %constant.8.clone.first_hbm, ...), custom_call_target="tpu_custom_call" | custom-call | tf_op jit(solution)/shard_map/pallas_call | solution.py:334
  21.9 1.7 %copy.13 = bf16[2,24,4,4,128]{4,3,2,1,0:T(4,128)(2,1)} copy(bf16[2,24,4,4,128]{4,3,2,1,0:T(4,128)(2,1)} %bitcast.1) | data formatting | bytes 393216

commit v2 on v1

--- a/solution.py
+++ b/solution.py
@@ -149,17 +149,24 @@
     sta = lax.axis_index("sta")
     freq = lax.axis_index("freq")
     core = lax.rem(freq, 2)
-    upper_chip = freq // 2
+    chip = freq // 2
     stride = n_sta // (2 * ROUNDS)
-
-    def block(steps):
-        return lax.rem(sta + (steps % 4) * stride, n_sta)
+    odd = lax.rem(sta // stride, 2)
+
+    def device(steps, index):
+        return {"sta": lax.rem(sta + (steps % 4) * stride, n_sta), "freq": index}
 
     barrier = pltpu.get_barrier_semaphore()
-    for steps, source in ((-1, 2), (-1, 3), (-2, 0), (-2, 1)):
-        pl.semaphore_signal(
-            barrier, inc=1, device_id={"sta": block(steps), "freq": source}, device_id_type=MESH
-        )
+
+    def signal(where):
+        pl.semaphore_signal(barrier, inc=1, device_id=where, device_id_type=MESH)
+
+    signal(device(-1, 3))
+    signal(device(-2, jnp.where(chip == 0, 2 + odd, 0)))
+
+    @pl.when(chip == 1)
+    def _():
+        signal(device(-2, 1))
 
     small = [
         pltpu.make_async_copy(source, target, load_sem.at[n])
@@ -185,39 +192,72 @@
             )
         )
     ]
+    feeds_next = (chip == 1) & (core == 1)
+    group = sta // stride
+    feeds_second = (chip == 1) & (core == 0) & (odd == 0) & (group != 0)
+    feeds_second_late = (chip == 1) & (core == 0) & (group == 0)
+    feeds_back = (chip == 0) & (odd == 0)
+    feeds_late = (chip == 0) & (odd == 1)
+    relays = feeds_back
+    expected = jnp.where(chip == 0, 2, jnp.where(core == 1, 4 + 2 * odd, 2))
+
+    @pl.when((chip == 0) | (core == 1) | (odd == 0))
+    def _():
+        pl.semaphore_wait(barrier, expected)
+
+    def wave_to(where, slot, place, order):
+        return pltpu.make_async_remote_copy(
+            src_ref=wave_hbm.at[slot],
+            dst_ref=far_wave_ref.at[place],
+            send_sem=send_sem.at[order],
+            recv_sem=recv_sem.at[place],
+            device_id=where,
+            device_id_type=MESH,
+        )
+
+    def about_to(where, slot, round_index, order):
+        return pltpu.make_async_remote_copy(
+            src_ref=about_ref.at[pl.ds(slot, 2)],
+            dst_ref=far_about_ref.at[round_index],
+            send_sem=send_sem.at[order],
+            recv_sem=recv_sem.at[4 + round_index],
+            device_id=where,
+            device_id_type=MESH,
+        )
+
+    def sends(steps, round_index):
+        targets = [device(steps, c) for c in range(2)]
+        return (
+            [wave_to(targets[c], 2 * c, 2 * round_index, c) for c in range(2)],
+            [about_to(targets[c], 2 * c, round_index, 4 + c) for c in range(2)]
+            + [wave_to(targets[c], 2 * c + 1, 2 * round_index + 1, 2 + c) for c in range(2)],
+        )
+
+    def sends_back():
+        target = device(2, 2 + core)
+        return (
+            [wave_to(target, 2 * core, 2, 0)],
+            [about_to(target, 2 * core, 1, 4), wave_to(target, 2 * core + 1, 3, 1)],
+        )
+
+    def start(copies):
+        for copy in copies:
+            copy.start()
+
+    @pl.when(feeds_next)
+    def _():
+        start(sends(1, 0)[0])
+
+    @pl.when(feeds_second)
+    def _():
+        start(sends(2, 1)[0])
+
+    @pl.when(feeds_back)
+    def _():
+        start(sends_back()[0])
+
     for copy in small + large:
         copy.start()
-
-    pl.semaphore_wait(barrier, 4)
-
-    feeds = {"sta": lax.rem(sta + (2 - upper_chip) * stride, n_sta), "freq": 2 * (1 - upper_chip) + core}
-
-    def send_wave(q):
-        return pltpu.make_async_remote_copy(
-            src_ref=wave_hbm.at[2 * core + q],
-            dst_ref=far_wave_ref.at[q],
-            send_sem=send_sem.at[q],
-            recv_sem=recv_sem.at[q],
-            device_id=feeds,
-            device_id_type=MESH,
-        )
-
-    def send_about():
-        return pltpu.make_async_remote_copy(
-            src_ref=about_ref.at[pl.ds(2 * core, 2)],
-            dst_ref=far_about_ref,
-            send_sem=send_sem.at[2],
-            recv_sem=recv_sem.at[2],
-            device_id=feeds,
-            device_id_type=MESH,
-        )
-
-    waits = (1 - upper_chip) * lax.rem(sta // stride, 2)
-
-    @pl.when(waits == 0)
-    def _():
-        send_wave(0).start()
-
     for copy in small:
         copy.wait()
 
@@ -233,18 +273,32 @@
             about_ref[slot, 8 + s : 9 + s, :] = jnp.full((1, ROOT), after.astype(jnp.float32), jnp.float32)
         about_ref[slot, 12:16, :] = jnp.zeros((4, ROOT), jnp.float32)
 
-    @pl.when(waits == 0)
-    def _():
-        send_about().start()
-        send_wave(1).start()
+    @pl.when(feeds_next)
+    def _():
+        start(sends(1, 0)[1])
+
+    @pl.when(feeds_second)
+    def _():
+        start(sends(2, 1)[1])
+
+    @pl.when(feeds_back)
+    def _():
+        start(sends_back()[1])
 
     for copy in large:
         copy.wait()
 
-    first_table = first_ref[...]
-    outer_table = outer_ref[...]
+    turn = jnp.where(group == 1, SLOTS - 1, 1)
 
     def own_step(slot, carry):
+        @pl.when(feeds_late & (slot == turn))
+        def _():
+            start(sends_back()[0] + sends_back()[1])
+
+        @pl.when(feeds_second_late & (slot == 1))
+        def _():
+            start(sends(2, 1)[0] + sends(2, 1)[1])
+
         found = spectra(
             wave_ref[slot], about_ref[slot], stage_ref, first_ref[...], twiddle_ref, square_ref
         )
@@ -254,29 +308,64 @@
 
     lax.fori_loop(0, SLOTS, own_step, 0)
 
-    @pl.when(waits == 1)
-    def _():
-        send_wave(0).start()
-        send_about().start()
-        send_wave(1).start()
-
-    def exchange(q, step):
-        target = lax.rem(freq + step, 4)
+    def relay(q):
+        copies = [
+            pltpu.make_async_remote_copy(
+                src_ref=far_wave_ref.at[q],
+                dst_ref=far_wave_ref.at[2 + q],
+                send_sem=send_sem.at[6 + q],
+                recv_sem=recv_sem.at[2 + q],
+                device_id=device(1, core),
+                device_id_type=MESH,
+            )
+        ]
+        if q == 0:
+            copies.append(
+                pltpu.make_async_remote_copy(
+                    src_ref=far_about_ref.at[0],
+                    dst_ref=far_about_ref.at[1],
+                    send_sem=send_sem.at[8],
+                    recv_sem=recv_sem.at[5],
+                    device_id=device(1, core),
+                    device_id_type=MESH,
+                )
+            )
+        return copies
+
+    def share(place, target):
         return pltpu.make_async_remote_copy(
-            src_ref=part_ref.at[q, target],
-            dst_ref=got_ref.at[upper_chip, 2 * core + q],
-            send_sem=part_send_sem.at[q, step],
-            recv_sem=part_recv_sem.at[q, step],
-            device_id={"sta": sta, "freq": target},
+            src_ref=part_ref.at[place, target],
+            dst_ref=got_ref.at[place // 2, 2 * core + lax.rem(place, 2)],
+            send_sem=part_send_sem.at[place, target],
+            recv_sem=part_recv_sem.at[place // 2, 2 * core + lax.rem(place, 2)],
+            device_id=device(0, target),
             device_id_type=MESH,
         )
 
-    for q in range(2):
-        if q == 0:
-            pltpu.make_async_copy(far_about_ref, far_about_ref, recv_sem.at[2]).wait()
-        pltpu.make_async_copy(far_wave_ref.at[q], far_wave_ref.at[q], recv_sem.at[q]).wait()
+    def far_step(place, carry):
+        round_index = place // 2
+        q = lax.rem(place, 2)
+
+        @pl.when(q == 0)
+        def _():
+            pltpu.make_async_copy(
+                far_about_ref.at[round_index], far_about_ref.at[round_index], recv_sem.at[4 + round_index]
+            ).wait()
+
+        pltpu.make_async_copy(far_wave_ref.at[place], far_wave_ref.at[place], recv_sem.at[place]).wait()
+        for early in range(2):
+
+            @pl.when(relays & (place == early))
+            def _(early=early):
+                start(relay(early))
+
         far = spectra(
-            far_wave_ref[q], far_about_ref[q], stage_ref, first_table, twiddle_ref, square_ref
+            far_wave_ref[place],
+            far_about_ref.at[round_index, q],
+            stage_ref,
+            first_ref[...],
+            twiddle_ref,
+            square_ref,
         )
         pairs = []
         for i in range(SLOTS):
@@ -299,36 +388,84 @@
                     [inner_re * cos_t - inner_im * sin_t, inner_re * sin_t + inner_im * cos_t], axis=0
                 ).astype(jnp.bfloat16)
             )
-        lagged = dot(outer_table, jnp.concatenate(columns, axis=1))
+        lagged = dot(outer_ref[...], jnp.concatenate(columns, axis=1))
         for g in range(4):
             band = lagged[g * BAND : (g + 1) * BAND]
-            part_ref[q, g] = jnp.concatenate(
+            part_ref[place, g] = jnp.concatenate(
                 [band[:, i * ROOT : (i + 1) * ROOT] for i in range(SLOTS)], axis=0
             ).astype(jnp.bfloat16)
-        for step in (2, 1, 3):
-            exchange(q, step).start()
-        got_ref[upper_chip, 2 * core + q] = part_ref[q, freq]
-
-    for q in range(2):
-        for step in (1, 2, 3):
-            exchange(q, step).wait_recv()
+
+        @pl.when(place < 2)
+        def _():
+            for target in (2, 3):
+                share(place, target).start()
+
+        share(place, freq + 1 - 2 * core).start()
+        got_ref[round_index, 2 * core + q] = part_ref[place, freq]
+        return carry
+
+    lax.fori_loop(2 * chip, 4, far_step, 0)
+
+    def arrived(round_index, slot):
+        pltpu.make_async_copy(
+            got_ref.at[round_index, slot], got_ref.at[round_index, slot], part_recv_sem.at[round_index, slot]
+        ).wait()
+
     for r in range(ROUNDS):
+        for q in range(2):
+            arrived(r, 2 * (1 - core) + q)
+        if r == 0:
+
+            @pl.when(chip == 1)
+            def _():
+                for q in range(2):
+                    arrived(0, 2 * core + q)
+
         for j in range(SLOTS):
             piece = got_ref[r, j].astype(jnp.float32)
             for i in range(SLOTS):
                 rows_ref[r, pl.ds(SLOTS * i + j, BAND, stride=SLOTS * SLOTS), :] = piece[i * BAND : (i + 1) * BAND]
         out_ref[r] = rows_ref[r].astype(jnp.bfloat16)
 
-    for q in range(2):
-        for step in (1, 2, 3):
-            exchange(q, step).wait_send()
-        send_wave(q).wait_send()
-    send_about().wait_send()
+    def finish(copies):
+        for copy in copies:
+            copy.wait_send()
+
+    def sent(place, carry):
+        @pl.when(place < 2)
+        def _():
+            for target in (2, 3):
+                share(place, target).wait_send()
+
+        share(place, freq + 1 - 2 * core).wait_send()
+        return carry
+
+    lax.fori_loop(2 * chip, 4, sent, 0)
+
+    @pl.when(feeds_next)
+    def _():
+        finish(sends(1, 0)[0] + sends(1, 0)[1])
+
+    @pl.when(feeds_second | feeds_second_late)
+    def _():
+        finish(sends(2, 1)[0] + sends(2, 1)[1])
+
+    @pl.when(chip == 0)
+    def _():
+        finish(sends_back()[0] + sends_back()[1])
+
+    @pl.when(relays)
+    def _():
+        finish(relay(0) + relay(1))
 
 
 def on_device(waveforms, fir_taps, water_level, gap_start, gap_length, live_slots):
     n_sta = lax.axis_size("sta")
     tables = [jnp.asarray(table) for table in make_tables()]
+
+    def pinned(*arrays):
+        return [pltpu.with_memory_space_constraint(array, pltpu.HBM) for array in arrays]
+
     anywhere = pl.BlockSpec(memory_space=pl.ANY)
     rows = BAND * SLOTS * SLOTS
     result = pl.pallas_call(
@@ -347,23 +484,25 @@
         + [pltpu.VMEM(table.shape, table.dtype) for table in tables]
         + [
             pltpu.VMEM((SLOTS, 16, ROOT), jnp.float32),
-            pltpu.VMEM((2, SEG, COARSE * ROOT), jnp.bfloat16),
-            pltpu.VMEM((2, 16, ROOT), jnp.float32),
+            pltpu.VMEM((4, SEG, COARSE * ROOT), jnp.bfloat16),
+            pltpu.VMEM((ROUNDS, 2, 16, ROOT), jnp.float32),
             pltpu.VMEM((SEG * COARSE, ROOT), jnp.float32),
             pltpu.VMEM((SLOTS, SEG, 2, KEPT, ROOT), jnp.float32),
-            pltpu.VMEM((2, 4, SLOTS * BAND, ROOT), jnp.bfloat16),
+            pltpu.VMEM((4, 4, SLOTS * BAND, ROOT), jnp.bfloat16),
             pltpu.VMEM((ROUNDS, SLOTS, SLOTS * BAND, ROOT), jnp.bfloat16),
             pltpu.VMEM((ROUNDS, rows, ROOT), jnp.float32),
             pltpu.SemaphoreType.DMA((10,)),
-            pltpu.SemaphoreType.DMA((3,)),
-            pltpu.SemaphoreType.DMA((3,)),
-            pltpu.SemaphoreType.DMA((2, 4)),
-            pltpu.SemaphoreType.DMA((2, 4)),
+            pltpu.SemaphoreType.DMA((9,)),
+            pltpu.SemaphoreType.DMA((6,)),
+            pltpu.SemaphoreType.DMA((4, 4)),
+            pltpu.SemaphoreType.DMA((ROUNDS, SLOTS)),
         ],
         compiler_params=pltpu.CompilerParams(
-            collective_id=0, has_side_effects=True, vmem_limit_bytes=56 * 1024 * 1024
+            collective_id=0, has_side_effects=True, vmem_limit_bytes=40 * 1024 * 1024
         ),
-    )(waveforms, fir_taps, water_level, gap_start, gap_length, live_slots, *tables)
+    )(
+        *pinned(waveforms, fir_taps, water_level, gap_start, gap_length), live_slots, *pinned(*tables)
+    )
     return result.reshape(ROUNDS, BAND, SLOTS, SLOTS, ROOT)
 
 

time: 23.7 us -> 19.9 us (0.84)
  the two profiles are of different devices: /device:TPU:65 before, /device:TPU:1 now
where the time goes in v2:
time: 19.9 us; the launch traced here: 19.7 us
  Pallas kernels  18.3 us (92%)
  local copies, waits for them, and re-layouts  0.68 us (3%)
  between operations  0.66 us (3%)
    pallas_call x1, Pallas kernels, on_device(): pl.pallas_call(functools.partial(kernel, n_sta), out_shape=jax.ShapeDtype...  18.3 us
    unnamed x1, local copies, waits for them, and re-layouts  0.68 us

profile of v2, /device:TPU:1, one launch (start us, length us, event | category | flops | bytes accessed | tf_op | source)
XLA Modules:
  0.0 19.7 jit_solution(17555867387221450292)
XLA Ops:
  0.7 18.3 %shard_map.100 = bf16[2,384,128]{2,1,0:T(8,128)(2,1)S(1)} custom-call(bf16[4,4,8192]{2,1,0:T(4,128)(2,1)} %wave_hbm.1, f32[4,256]{1,0:T(4,128)} %taps_hbm.1, f32[4]{0:T(128)} %water_hbm.1, s32[4,4]{1,0:T(4,128)} %start_hbm.1, s32[4,4]{1,0:T(4,128)} %length_hbm.1, s32[1]{0:T(128)S(6)} %copy.12.live_hbm, bf16[144,128]{1,0:T(8,128)(2,1)} %constant.8.clone.first_hbm, ...), custom_call_target="tpu_custom_call" | custom-call | tf_op jit(solution)/shard_map/pallas_call | solution.py:471
  19.0 0.7 %copy.13 = bf16[2,24,4,4,128]{4,3,2,1,0:T(4,128)(2,1)} copy(bf16[2,24,4,4,128]{4,3,2,1,0:T(4,128)(2,1)S(1)} %bitcast.1) | data formatting | bytes 393216

commit v3 on v1

--- a/solution.py
+++ b/solution.py
@@ -143,23 +143,19 @@
     load_sem,
     send_sem,
     recv_sem,
+    about_sem,
     part_send_sem,
     part_recv_sem,
 ):
     sta = lax.axis_index("sta")
     freq = lax.axis_index("freq")
     core = lax.rem(freq, 2)
-    upper_chip = freq // 2
+    chip = freq // 2
     stride = n_sta // (2 * ROUNDS)
-
-    def block(steps):
-        return lax.rem(sta + (steps % 4) * stride, n_sta)
-
-    barrier = pltpu.get_barrier_semaphore()
-    for steps, source in ((-1, 2), (-1, 3), (-2, 0), (-2, 1)):
-        pl.semaphore_signal(
-            barrier, inc=1, device_id={"sta": block(steps), "freq": source}, device_id_type=MESH
-        )
+    odd = lax.rem(sta // stride, 2)
+
+    def device(steps, index):
+        return {"sta": lax.rem(sta + (steps % 4) * stride, n_sta), "freq": index}
 
     small = [
         pltpu.make_async_copy(source, target, load_sem.at[n])
@@ -185,38 +181,69 @@
             )
         )
     ]
-    for copy in small + large:
+    barrier = pltpu.get_barrier_semaphore()
+    for copy in small:
         copy.start()
-
-    pl.semaphore_wait(barrier, 4)
-
-    feeds = {"sta": lax.rem(sta + (2 - upper_chip) * stride, n_sta), "freq": 2 * (1 - upper_chip) + core}
-
-    def send_wave(q):
+    for c in range(2):
+        pl.semaphore_signal(barrier, inc=1, device_id=device(-1, 2 + c), device_id_type=MESH)
+        pl.semaphore_signal(barrier, inc=1, device_id=device(-2, 2 * (1 - chip) + c), device_id_type=MESH)
+
+    group = sta // stride
+    pl.semaphore_wait(barrier, 2 + 4 * chip)
+
+    def send(source, slot, target, place, where, order):
         return pltpu.make_async_remote_copy(
-            src_ref=wave_hbm.at[2 * core + q],
-            dst_ref=far_wave_ref.at[q],
-            send_sem=send_sem.at[q],
-            recv_sem=recv_sem.at[q],
-            device_id=feeds,
+            src_ref=source.at[slot],
+            dst_ref=target.at[place],
+            send_sem=send_sem.at[order],
+            recv_sem=(recv_sem if target is far_wave_ref else about_sem).at[place],
+            device_id=where,
             device_id_type=MESH,
         )
 
-    def send_about():
-        return pltpu.make_async_remote_copy(
-            src_ref=about_ref.at[pl.ds(2 * core, 2)],
-            dst_ref=far_about_ref,
-            send_sem=send_sem.at[2],
-            recv_sem=recv_sem.at[2],
-            device_id=feeds,
-            device_id_type=MESH,
-        )
-
-    waits = (1 - upper_chip) * lax.rem(sta // stride, 2)
-
-    @pl.when(waits == 0)
-    def _():
-        send_wave(0).start()
+    def next_sends(source, target, order):
+        return [
+            send(source, 2 * other + core, target, 0, device(1, 2 * other + core), order + other)
+            for other in (1, 0)
+        ]
+
+    def second_sends(source, target, order):
+        where = device(2, 2 * (1 - chip) + core)
+        return [send(source, 2 * n + core, target, 1 + n, where, order + n) for n in range(2)]
+
+    def next_waves():
+        return next_sends(wave_hbm, far_wave_ref, 0)
+
+    def next_abouts():
+        return next_sends(about_ref, far_about_ref, 2)
+
+    def second_waves():
+        return second_sends(wave_hbm, far_wave_ref, 4)
+
+    def second_abouts():
+        return second_sends(about_ref, far_about_ref, 6)
+
+    def relay():
+        where = device(1, core)
+        return [
+            send(far_wave_ref, 0, far_wave_ref, 1 + chip, where, 8),
+            send(far_about_ref, 0, far_about_ref, 1 + chip, where, 9),
+        ]
+
+    def start(copies):
+        for copy in copies:
+            copy.start()
+
+    relays = group != 3
+    feeds_second = (chip == 0) | (group == 2)
+
+    @pl.when((chip == 1) & (group != 2))
+    def _():
+        start(next_waves())
+
+    @pl.when((chip == 0) & (odd == 0))
+    def _():
+        start(second_waves())
 
     for copy in small:
         copy.wait()
@@ -233,18 +260,31 @@
             about_ref[slot, 8 + s : 9 + s, :] = jnp.full((1, ROOT), after.astype(jnp.float32), jnp.float32)
         about_ref[slot, 12:16, :] = jnp.zeros((4, ROOT), jnp.float32)
 
-    @pl.when(waits == 0)
-    def _():
-        send_about().start()
-        send_wave(1).start()
-
+    @pl.when(chip == 1)
+    def _():
+        start(next_abouts())
+
+    @pl.when(feeds_second)
+    def _():
+        start(second_abouts())
+
+    for copy in large:
+        copy.start()
     for copy in large:
         copy.wait()
 
-    first_table = first_ref[...]
-    outer_table = outer_ref[...]
+    turn = jnp.where((chip == 0) & (group == 1), SLOTS - 1, 0)
+    later = feeds_second & jnp.logical_not((chip == 0) & (odd == 0))
 
     def own_step(slot, carry):
+        @pl.when((chip == 1) & (group == 2) & (slot == 2))
+        def _():
+            start(next_waves())
+
+        @pl.when(later & (slot == turn))
+        def _():
+            start(second_waves())
+
         found = spectra(
             wave_ref[slot], about_ref[slot], stage_ref, first_ref[...], twiddle_ref, square_ref
         )
@@ -254,29 +294,34 @@
 
     lax.fori_loop(0, SLOTS, own_step, 0)
 
-    @pl.when(waits == 1)
-    def _():
-        send_wave(0).start()
-        send_about().start()
-        send_wave(1).start()
-
-    def exchange(q, step):
-        target = lax.rem(freq + step, 4)
+    def slot_of(place):
+        return jnp.where(place == 0, freq, core + 2 * (place - 1))
+
+    def share(place, target):
         return pltpu.make_async_remote_copy(
-            src_ref=part_ref.at[q, target],
-            dst_ref=got_ref.at[upper_chip, 2 * core + q],
-            send_sem=part_send_sem.at[q, step],
-            recv_sem=part_recv_sem.at[q, step],
-            device_id={"sta": sta, "freq": target},
+            src_ref=part_ref.at[place, target],
+            dst_ref=got_ref.at[jnp.minimum(place, 1), slot_of(place)],
+            send_sem=part_send_sem.at[place, target],
+            recv_sem=part_recv_sem.at[jnp.minimum(place, 1), slot_of(place)],
+            device_id=device(0, target),
             device_id_type=MESH,
         )
 
-    for q in range(2):
-        if q == 0:
-            pltpu.make_async_copy(far_about_ref, far_about_ref, recv_sem.at[2]).wait()
-        pltpu.make_async_copy(far_wave_ref.at[q], far_wave_ref.at[q], recv_sem.at[q]).wait()
+    def far_step(place, carry):
+        pltpu.make_async_copy(far_wave_ref.at[place], far_wave_ref.at[place], recv_sem.at[place]).wait()
+        pltpu.make_async_copy(far_about_ref.at[place], far_about_ref.at[place], about_sem.at[place]).wait()
+
+        @pl.when(relays & (place == 0))
+        def _():
+            start(relay())
+
         far = spectra(
-            far_wave_ref[q], far_about_ref[q], stage_ref, first_table, twiddle_ref, square_ref
+            far_wave_ref[place],
+            far_about_ref.at[place],
+            stage_ref,
+            first_ref[...],
+            twiddle_ref,
+            square_ref,
         )
         pairs = []
         for i in range(SLOTS):
@@ -299,36 +344,68 @@
                     [inner_re * cos_t - inner_im * sin_t, inner_re * sin_t + inner_im * cos_t], axis=0
                 ).astype(jnp.bfloat16)
             )
-        lagged = dot(outer_table, jnp.concatenate(columns, axis=1))
+        lagged = dot(outer_ref[...], jnp.concatenate(columns, axis=1))
         for g in range(4):
             band = lagged[g * BAND : (g + 1) * BAND]
-            part_ref[q, g] = jnp.concatenate(
+            part_ref[place, g] = jnp.concatenate(
                 [band[:, i * ROOT : (i + 1) * ROOT] for i in range(SLOTS)], axis=0
             ).astype(jnp.bfloat16)
-        for step in (2, 1, 3):
-            exchange(q, step).start()
-        got_ref[upper_chip, 2 * core + q] = part_ref[q, freq]
-
-    for q in range(2):
-        for step in (1, 2, 3):
-            exchange(q, step).wait_recv()
+
+        @pl.when(place == 0)
+        def _():
+            for c in range(2):
+                share(place, 2 * (1 - chip) + c).start()
+
+        share(place, freq + 1 - 2 * core).start()
+        got_ref[jnp.minimum(place, 1), slot_of(place)] = part_ref[place, freq]
+        return carry
+
+    lax.fori_loop(0, 3, far_step, 0)
+
+    def arrived(round_index, slot):
+        pltpu.make_async_copy(
+            got_ref.at[round_index, slot], got_ref.at[round_index, slot], part_recv_sem.at[round_index, slot]
+        ).wait()
+
     for r in range(ROUNDS):
+        for slot in [lax.rem(freq + step, 4) for step in range(1, 4)] if r == 0 else [1 - core, 3 - core]:
+            arrived(r, slot)
+
         for j in range(SLOTS):
             piece = got_ref[r, j].astype(jnp.float32)
             for i in range(SLOTS):
-                rows_ref[r, pl.ds(SLOTS * i + j, BAND, stride=SLOTS * SLOTS), :] = piece[i * BAND : (i + 1) * BAND]
-        out_ref[r] = rows_ref[r].astype(jnp.bfloat16)
-
-    for q in range(2):
-        for step in (1, 2, 3):
-            exchange(q, step).wait_send()
-        send_wave(q).wait_send()
-    send_about().wait_send()
+                rows_ref[pl.ds(SLOTS * i + j, BAND, stride=SLOTS * SLOTS), :] = piece[i * BAND : (i + 1) * BAND]
+        out_ref[r] = rows_ref[...].astype(jnp.bfloat16)
+
+    def finish(copies):
+        for copy in copies:
+            copy.wait_send()
+
+    for c in range(2):
+        share(0, 2 * (1 - chip) + c).wait_send()
+    for place in range(3):
+        share(place, freq + 1 - 2 * core).wait_send()
+
+    @pl.when(chip == 1)
+    def _():
+        finish(next_waves() + next_abouts())
+
+    @pl.when(feeds_second)
+    def _():
+        finish(second_waves() + second_abouts())
+
+    @pl.when(relays)
+    def _():
+        finish(relay())
 
 
 def on_device(waveforms, fir_taps, water_level, gap_start, gap_length, live_slots):
     n_sta = lax.axis_size("sta")
     tables = [jnp.asarray(table) for table in make_tables()]
+
+    def pinned(*arrays):
+        return [pltpu.with_memory_space_constraint(array, pltpu.HBM) for array in arrays]
+
     anywhere = pl.BlockSpec(memory_space=pl.ANY)
     rows = BAND * SLOTS * SLOTS
     result = pl.pallas_call(
@@ -347,23 +424,26 @@
         + [pltpu.VMEM(table.shape, table.dtype) for table in tables]
         + [
             pltpu.VMEM((SLOTS, 16, ROOT), jnp.float32),
-            pltpu.VMEM((2, SEG, COARSE * ROOT), jnp.bfloat16),
-            pltpu.VMEM((2, 16, ROOT), jnp.float32),
+            pltpu.VMEM((3, SEG, COARSE * ROOT), jnp.bfloat16),
+            pltpu.VMEM((3, 16, ROOT), jnp.float32),
             pltpu.VMEM((SEG * COARSE, ROOT), jnp.float32),
             pltpu.VMEM((SLOTS, SEG, 2, KEPT, ROOT), jnp.float32),
-            pltpu.VMEM((2, 4, SLOTS * BAND, ROOT), jnp.bfloat16),
+            pltpu.VMEM((3, 4, SLOTS * BAND, ROOT), jnp.bfloat16),
             pltpu.VMEM((ROUNDS, SLOTS, SLOTS * BAND, ROOT), jnp.bfloat16),
-            pltpu.VMEM((ROUNDS, rows, ROOT), jnp.float32),
+            pltpu.VMEM((rows, ROOT), jnp.float32),
+            pltpu.SemaphoreType.DMA((10,)),
             pltpu.SemaphoreType.DMA((10,)),
             pltpu.SemaphoreType.DMA((3,)),
             pltpu.SemaphoreType.DMA((3,)),
-            pltpu.SemaphoreType.DMA((2, 4)),
-            pltpu.SemaphoreType.DMA((2, 4)),
+            pltpu.SemaphoreType.DMA((3, 4)),
+            pltpu.SemaphoreType.DMA((ROUNDS, SLOTS)),
         ],
         compiler_params=pltpu.CompilerParams(
-            collective_id=0, has_side_effects=True, vmem_limit_bytes=56 * 1024 * 1024
+            collective_id=0, has_side_effects=True, vmem_limit_bytes=40 * 1024 * 1024
         ),
-    )(waveforms, fir_taps, water_level, gap_start, gap_length, live_slots, *tables)
+    )(
+        *pinned(waveforms, fir_taps, water_level, gap_start, gap_length), live_slots, *pinned(*tables)
+    )
     return result.reshape(ROUNDS, BAND, SLOTS, SLOTS, ROOT)
 
 

time: 23.7 us -> 19.4 us (0.82)
  the two profiles are of different devices: /device:TPU:65 before, /device:TPU:1 now
where the time goes in v3:
time: 19.4 us; the launch traced here: 19.2 us
  Pallas kernels  17.9 us (92%)
  local copies, waits for them, and re-layouts  0.68 us (4%)
  between operations  0.66 us (3%)
    pallas_call x1, Pallas kernels, on_device(): pl.pallas_call(functools.partial(kernel, n_sta), out_shape=jax.ShapeDtype...  17.9 us
    unnamed x1, local copies, waits for them, and re-layouts  0.68 us

profile of v3, /device:TPU:1, one launch (start us, length us, event | category | flops | bytes accessed | tf_op | source)
XLA Modules:
  0.0 19.2 jit_solution(13991426145341746952)
XLA Ops:
  0.7 17.9 %shard_map.100 = bf16[2,384,128]{2,1,0:T(8,128)(2,1)S(1)} custom-call(bf16[4,4,8192]{2,1,0:T(4,128)(2,1)} %wave_hbm.1, f32[4,256]{1,0:T(4,128)} %taps_hbm.1, f32[4]{0:T(128)} %water_hbm.1, s32[4,4]{1,0:T(4,128)} %start_hbm.1, s32[4,4]{1,0:T(4,128)} %length_hbm.1, s32[1]{0:T(128)S(6)} %copy.12.live_hbm, bf16[144,128]{1,0:T(8,128)(2,1)} %constant.8.clone.first_hbm, ...), custom_call_target="tpu_custom_call" | custom-call | tf_op jit(solution)/shard_map/pallas_call | solution.py:411
  18.5 0.7 %copy.13 = bf16[2,24,4,4,128]{4,3,2,1,0:T(4,128)(2,1)} copy(bf16[2,24,4,4,128]{4,3,2,1,0:T(4,128)(2,1)S(1)} %bitcast.1) | data formatting | bytes 393216

commit v4 on v3

--- a/solution.py
+++ b/solution.py
@@ -307,6 +307,13 @@
             device_id_type=MESH,
         )
 
+    def lay(round_index, slot, block):
+        piece = block.astype(jnp.float32)
+        for i in range(SLOTS):
+            rows_ref[round_index, pl.ds(SLOTS * i + slot, BAND, stride=SLOTS * SLOTS), :] = piece[
+                i * BAND : (i + 1) * BAND
+            ]
+
     def far_step(place, carry):
         pltpu.make_async_copy(far_wave_ref.at[place], far_wave_ref.at[place], recv_sem.at[place]).wait()
         pltpu.make_async_copy(far_about_ref.at[place], far_about_ref.at[place], about_sem.at[place]).wait()
@@ -357,7 +364,7 @@
                 share(place, 2 * (1 - chip) + c).start()
 
         share(place, freq + 1 - 2 * core).start()
-        got_ref[jnp.minimum(place, 1), slot_of(place)] = part_ref[place, freq]
+        lay(jnp.minimum(place, 1), slot_of(place), part_ref[place, freq])
         return carry
 
     lax.fori_loop(0, 3, far_step, 0)
@@ -368,14 +375,11 @@
         ).wait()
 
     for r in range(ROUNDS):
-        for slot in [lax.rem(freq + step, 4) for step in range(1, 4)] if r == 0 else [1 - core, 3 - core]:
+        others = [freq + 1 - 2 * core, 2 * (1 - chip), 2 * (1 - chip) + 1] if r == 0 else [1 - core, 3 - core]
+        for slot in others:
             arrived(r, slot)
-
-        for j in range(SLOTS):
-            piece = got_ref[r, j].astype(jnp.float32)
-            for i in range(SLOTS):
-                rows_ref[pl.ds(SLOTS * i + j, BAND, stride=SLOTS * SLOTS), :] = piece[i * BAND : (i + 1) * BAND]
-        out_ref[r] = rows_ref[...].astype(jnp.bfloat16)
+            lay(r, slot, got_ref[r, slot])
+        out_ref[r] = rows_ref[r].astype(jnp.bfloat16)
 
     def finish(copies):
         for copy in copies:
@@ -430,7 +434,7 @@
             pltpu.VMEM((SLOTS, SEG, 2, KEPT, ROOT), jnp.float32),
             pltpu.VMEM((3, 4, SLOTS * BAND, ROOT), jnp.bfloat16),
             pltpu.VMEM((ROUNDS, SLOTS, SLOTS * BAND, ROOT), jnp.bfloat16),
-            pltpu.VMEM((rows, ROOT), jnp.float32),
+            pltpu.VMEM((ROUNDS, rows, ROOT), jnp.float32),
             pltpu.SemaphoreType.DMA((10,)),
             pltpu.SemaphoreType.DMA((10,)),
             pltpu.SemaphoreType.DMA((3,)),

time: 19.4 us -> 19.3 us (level)
  no operation moved by 1% of the time
where the time goes in v4:
time: 19.3 us; the launch traced here: 19.2 us
  Pallas kernels  17.8 us (92%)
  local copies, waits for them, and re-layouts  0.68 us (4%)
  between operations  0.66 us (3%)
    pallas_call x1, Pallas kernels, on_device(): pl.pallas_call(functools.partial(kernel, n_sta), out_shape=jax.ShapeDtype...  17.8 us
    unnamed x1, local copies, waits for them, and re-layouts  0.68 us

profile of v4, /device:TPU:1, one launch (start us, length us, event | category | flops | bytes accessed | tf_op | source)
XLA Modules:
  0.0 19.2 jit_solution(3857924647345672107)
XLA Ops:
  0.7 17.8 %shard_map.100 = bf16[2,384,128]{2,1,0:T(8,128)(2,1)S(1)} custom-call(bf16[4,4,8192]{2,1,0:T(4,128)(2,1)} %wave_hbm.1, f32[4,256]{1,0:T(4,128)} %taps_hbm.1, f32[4]{0:T(128)} %water_hbm.1, s32[4,4]{1,0:T(4,128)} %start_hbm.1, s32[4,4]{1,0:T(4,128)} %length_hbm.1, s32[1]{0:T(128)S(6)} %copy.12.live_hbm, bf16[144,128]{1,0:T(8,128)(2,1)} %constant.8.clone.first_hbm, ...), custom_call_target="tpu_custom_call" | custom-call | tf_op jit(solution)/shard_map/pallas_call | solution.py:415
  18.5 0.7 %copy.13 = bf16[2,24,4,4,128]{4,3,2,1,0:T(4,128)(2,1)} copy(bf16[2,24,4,4,128]{4,3,2,1,0:T(4,128)(2,1)S(1)} %bitcast.1) | data formatting | bytes 393216

commit v5 on v4

--- a/solution.py
+++ b/solution.py
@@ -352,11 +352,18 @@
                 ).astype(jnp.bfloat16)
             )
         lagged = dot(outer_ref[...], jnp.concatenate(columns, axis=1))
-        for g in range(4):
+        def keep(g):
             band = lagged[g * BAND : (g + 1) * BAND]
             part_ref[place, g] = jnp.concatenate(
                 [band[:, i * ROOT : (i + 1) * ROOT] for i in range(SLOTS)], axis=0
             ).astype(jnp.bfloat16)
+
+        for half in range(2):
+
+            @pl.when((place == 0) | (chip == half))
+            def _(half=half):
+                keep(2 * half)
+                keep(2 * half + 1)
 
         @pl.when(place == 0)
         def _():

time: 19.3 us -> 19.3 us (level)
  no operation moved by 1% of the time
where the time goes in v5:
time: 19.3 us; the launch traced here: 19.2 us
  Pallas kernels  17.9 us (93%)
  local copies, waits for them, and re-layouts  0.68 us (4%)
  between operations  0.66 us (3%)
    pallas_call x1, Pallas kernels, on_device(): pl.pallas_call(functools.partial(kernel, n_sta), out_shape=jax.ShapeDtype...  17.9 us
    unnamed x1, local copies, waits for them, and re-layouts  0.68 us

profile of v5, /device:TPU:1, one launch (start us, length us, event | category | flops | bytes accessed | tf_op | source)
XLA Modules:
  0.0 19.2 jit_solution(13726242565471420089)
XLA Ops:
  0.7 17.9 %shard_map.100 = bf16[2,384,128]{2,1,0:T(8,128)(2,1)S(1)} custom-call(bf16[4,4,8192]{2,1,0:T(4,128)(2,1)} %wave_hbm.1, f32[4,256]{1,0:T(4,128)} %taps_hbm.1, f32[4]{0:T(128)} %water_hbm.1, s32[4,4]{1,0:T(4,128)} %start_hbm.1, s32[4,4]{1,0:T(4,128)} %length_hbm.1, s32[1]{0:T(128)S(6)} %copy.12.live_hbm, bf16[144,128]{1,0:T(8,128)(2,1)} %constant.8.clone.first_hbm, ...), custom_call_target="tpu_custom_call" | custom-call | tf_op jit(solution)/shard_map/pallas_call | solution.py:422
  18.5 0.7 %copy.13 = bf16[2,24,4,4,128]{4,3,2,1,0:T(4,128)(2,1)} copy(bf16[2,24,4,4,128]{4,3,2,1,0:T(4,128)(2,1)S(1)} %bitcast.1) | data formatting | bytes 393216
